TPU v7x, 32 devices: a whole 2x2x4 slice. The times are simulated.
32 devices in a mesh: seq: 8 (over z, x), head: 4 (over y, core).
Axes of the slice: x: 2, y: 2, z: 4, core: 2. Of those that a mesh axis runs over, the one named last changes fastest.
Arguments:
- query: bfloat16 [16384, 1024], P('seq', 'head'), may hold values from -9 to 9
- key: bfloat16 [16384, 1024], P('seq', 'head'), may hold values from -9 to 9
- value: bfloat16 [16384, 1024], P('seq', 'head'), may hold values from -6 to 6
- offsets: int32 [5, 16], P(None, 'head'), may hold values from 0 to 15, as said below
Outputs:
- attended: bfloat16 [16384, 1024], P('seq', 'head')
Inputs may be any that keep to these rules, and one draw needn't show every extreme that they name: offsets[0, h] is 0; offsets[l, h] lies below the rate of level l: 1, 4, 4, 4, 16; at every level some head takes the largest value.
All inputs are finite; a program needn't handle non-finite values.
Results may differ from a plain program's by a relative error of at most 0.0046.
Values may be sent and summed in bfloat16 or wider, within the bound.
A program may use at most 320 MiB of HBM per device.

v0:
```python
import functools

import jax
import jax.numpy as jnp
from jax import lax
from jax.experimental import pallas as pl
from jax.experimental.pallas import tpu as pltpu
from jax.sharding import PartitionSpec as P

SEG = 512
RATE1 = 4
NEG = -1e30
LANES = 128
BF = jnp.bfloat16
F32 = jnp.float32
MESH = pl.DeviceIdType.MESH


def flip(me, i, bits):
    out = me
    for b in range(bits):
        w = 1 << b
        mine = lax.rem(lax.div(me, w), 2)
        want = lax.rem(lax.div(jnp.int32(i), w), 2)
        out = out + want * w * (1 - 2 * mine)
    return out


def half_roll(x):
    return pltpu.roll(x, LANES // 2, 1)


def tile_of(rate):
    return 16 * max(rate, 16)


def dot(a, b):
    return jnp.dot(a, b, preferred_element_type=F32)


def dot_t(a, b):
    return lax.dot_general(a, b, (((1,), (1,)), ((), ())), preferred_element_type=F32)


def attention(q, k, v_one):
    s = dot_t(q, k)
    top = jnp.max(s, axis=1, keepdims=True)
    p = jnp.exp(s - top).astype(BF)
    return dot(p, v_one), top


def kernel(cfg, q_ref, k_ref, v_ref, offs_ref, out_ref, *scratch):
    rates, counts, fars, heads, rows, width = cfg
    levels = (2, 3, 4)
    names = ("qs", "kvs", "qr", "kv", "kv1", "os", "ls", "ro", "rl")
    bufs = {}
    pos = 0
    for l in levels:
        for nm in names:
            bufs[nm, l] = scratch[pos]
            pos += 1
    (q1, k1, v1, out_l1, lse_buf, out_buf, num, tot, mx, sq, rq, skv, rkv, so, ro_s, sl, rl_s, sfar, rfar) = scratch[pos:]

    me = lax.axis_index("seq")
    hd = lax.axis_index("head")
    gbits = heads.bit_length() - 1
    mine = lax.rem(me, heads)
    nfar = max(fars.values())
    pairs = width // LANES
    scale = (width // heads) ** (-0.5)

    def dev(i):
        return (flip(me, i, gbits), hd)

    def far_dev(b):
        return (flip(me, heads << b, gbits + b + 1), hd)

    barrier = pltpu.get_barrier_semaphore()
    for i in range(1, heads):
        pl.semaphore_signal(barrier, inc=1, device_id=dev(i), device_id_type=MESH)
    for b in range(nfar):
        pl.semaphore_signal(barrier, inc=1, device_id=far_dev(b), device_id_type=MESH)

    low = lax.broadcasted_iota(jnp.int32, (1, LANES), 1) < LANES // 2
    low_f = jnp.where(low, 1.0, 0.0)
    low_b = low_f.astype(BF)
    high_b = (1.0 - low_f).astype(BF)

    def chooser(rate, tile):
        g = tile // rate
        r = lax.broadcasted_iota(jnp.int32, (g, tile), 0)
        c = lax.broadcasted_iota(jnp.int32, (g, tile), 1)
        return jnp.where((c >= r * rate) & (c < (r + 1) * rate), 1.0, 0.0).astype(BF)

    def spreader(rate, tile, copies):
        g = tile // rate
        r = lax.broadcasted_iota(jnp.int32, (tile, g), 0)
        c = lax.broadcasted_iota(jnp.int32, (tile, g), 1)
        one = jnp.where((r >= c * rate) & (r < (c + 1) * rate), 1.0, 0.0)
        return jnp.concatenate([one] * copies, axis=1).astype(BF) if copies > 1 else one.astype(BF)

    def hits(l, rate, tile):
        r = lax.broadcasted_iota(jnp.int32, (tile, width), 0) & (rate - 1)
        return r == offs_ref[l : l + 1, :]

    def halves(a, b):
        return jnp.where(low, a, half_roll(b)), jnp.where(low, half_roll(a), b)

    def picker(l, rate):
        tile = tile_of(rate)
        choose = chooser(rate, tile)
        mask = jnp.where(hits(l, rate, tile), 1.0, 0.0).astype(BF)

        def pick(ref, t):
            return dot(choose, ref[pl.ds(pl.multiple_of(t * tile, tile), tile), :] * mask)

        return pick, tile, tile // rate, rows // tile

    def pack(l):
        pick, tile, g, steps = picker(l, rates[l])
        half = steps // 2
        qs, kvs = bufs["qs", l], bufs["kvs", l]

        def body(t, _):
            qa, qb = pick(q_ref, t), pick(q_ref, t + half)
            at = pl.ds(pl.multiple_of(t * g, g), g)
            for p in range(pairs):
                cut = slice(p * LANES, (p + 1) * LANES)
                a, b = halves(qa[:, cut], qb[:, cut])
                qs[2 * p, at, :] = a.astype(BF)
                qs[2 * p + 1, at, :] = b.astype(BF)
            for u in (t, t + half):
                kk, vv = pick(k_ref, u), pick(v_ref, u)
                at2 = pl.ds(pl.multiple_of(u * g, g), g)
                for p in range(pairs):
                    cut = slice(p * LANES, (p + 1) * LANES)
                    a, b = halves(kk[:, cut], vv[:, cut])
                    kvs[2 * p, at2, :] = a.astype(BF)
                    kvs[2 * p + 1, at2, :] = b.astype(BF)
            return 0

        lax.fori_loop(0, half, body, 0)

    def copies_in(l, i):
        n = counts[l]
        to = flip(mine, i, gbits)
        a = pltpu.make_async_remote_copy(
            src_ref=bufs["kvs", l].at[to], dst_ref=bufs["kv", l].at[pl.ds(i * n, n)],
            send_sem=skv.at[l - 2, i], recv_sem=rkv.at[l - 2, i], device_id=dev(i), device_id_type=MESH)
        b = pltpu.make_async_remote_copy(
            src_ref=bufs["qs", l].at[to], dst_ref=bufs["qr", l].at[i],
            send_sem=sq.at[l - 2, i], recv_sem=rq.at[l - 2, i], device_id=dev(i), device_id_type=MESH)
        return a, b

    def copies_back(l, i, slot):
        a = pltpu.make_async_remote_copy(
            src_ref=bufs["os", l].at[i], dst_ref=bufs["ro", l].at[slot],
            send_sem=so.at[l - 2, i], recv_sem=ro_s.at[l - 2, i], device_id=dev(i), device_id_type=MESH)
        b = pltpu.make_async_remote_copy(
            src_ref=bufs["ls", l].at[i], dst_ref=bufs["rl", l].at[slot],
            send_sem=sl.at[l - 2, i], recv_sem=rl_s.at[l - 2, i], device_id=dev(i), device_id_type=MESH)
        return a, b

    def copy_far(l, b):
        n = heads * counts[l] << b
        return pltpu.make_async_remote_copy(
            src_ref=bufs["kv", l].at[pl.ds(0, n)], dst_ref=bufs["kv", l].at[pl.ds(n, n)],
            send_sem=sfar.at[l - 2, b], recv_sem=rfar.at[l - 2, b], device_id=far_dev(b), device_id_type=MESH)

    first = True
    for l in (2, 4, 3):
        pack(l)
        if first:
            pl.semaphore_wait(barrier, heads - 1 + nfar)
            first = False
        for i in range(1, heads):
            for c in copies_in(l, i):
                c.start()
        bufs["kv", l][0 : counts[l], :] = bufs["kvs", l][mine]
        bufs["qr", l][0] = bufs["qs", l][mine]

    def pair_attention(qv, kv, vv):
        o0, m0 = attention(qv * (low_b * scale).astype(BF), kv, vv * low_b + high_b)
        o1, m1 = attention(qv * (high_b * scale).astype(BF), kv, vv * high_b + low_b)
        return (
            jnp.where(low, o0, o1),
            half_roll(jnp.where(low, o1, o0)),
            jnp.where(low, m0, m1),
        )

    qt = SEG // 2

    def first_level(t, _):
        at = pl.ds(pl.multiple_of(t * qt, qt), qt)
        keys = pl.ds(pl.multiple_of(lax.div(t, SEG // qt) * SEG, SEG), SEG)
        for p in range(pairs):
            cut = slice(p * LANES, (p + 1) * LANES)
            a, b, c = pair_attention(q_ref[at, cut], k_ref[keys, cut], v_ref[keys, cut])
            num[at, cut] = a
            tot[at, cut] = b
            mx[at, cut] = c
        return 0

    lax.fori_loop(0, rows // qt, first_level, 0)

    pick, tile, g, steps = picker(1, RATE1)

    def pick_one(t, _):
        at = pl.ds(pl.multiple_of(t * g, g), g)
        for src, dst in ((q_ref, q1), (k_ref, k1), (v_ref, v1)):
            dst[at, :] = pick(src, t).astype(BF)
        return 0

    lax.fori_loop(0, steps, pick_one, 0)

    def second_level(t, _):
        at = pl.ds(pl.multiple_of(t * qt, qt), qt)
        for p in range(pairs):
            cut = slice(p * LANES, (p + 1) * LANES)
            a, b, c = pair_attention(q1[at, cut], k1[:, cut], v1[:, cut])
            out_l1[at, cut] = a / b
            lse_buf[at, cut] = c + jnp.log(b)
        return 0

    lax.fori_loop(0, rows // RATE1 // qt, second_level, 0)

    def merge(l, rate, source, last):
        tile = tile_of(rate)
        g = tile // rate
        fine = source.dtype == F32
        s_out = spreader(rate, tile, 2 if fine else 1)
        s_lse = spreader(rate, tile, 3)
        hit = hits(l, rate, tile)

        def body(t, _):
            at = pl.ds(pl.multiple_of(t * tile, tile), tile)
            pt = pl.ds(pl.multiple_of(t * g, g), g)
            o = source[pt, :]
            if fine:
                hi = o.astype(BF).astype(F32)
                o = jnp.concatenate([hi, o - hi], axis=0).astype(BF)
            e = lse_buf[pt, :]
            e0 = e.astype(BF).astype(F32)
            e1 = (e - e0).astype(BF).astype(F32)
            e2 = e - e0 - e1
            x = dot(s_out, o)
            y = dot(s_lse, jnp.concatenate([e0, e1, e2], axis=0).astype(BF))
            y = jnp.where(hit, y, NEG)
            old = mx[at, :]
            new = jnp.maximum(old, y)
            a, b = jnp.exp(old - new), jnp.exp(y - new)
            nn = num[at, :] * a + x * b
            tt = tot[at, :] * a + b
            if last:
                out_ref[at, :] = (nn / tt).astype(BF)
            else:
                num[at, :] = nn
                tot[at, :] = tt
                mx[at, :] = new
            return 0

        lax.fori_loop(0, rows // tile, body, 0)

    merge(1, RATE1, out_l1, False)

    def arrive(l):
        for i in range(1, heads):
            for c in copies_in(l, i):
                c.wait_recv()

    def work(l):
        n = counts[l]
        h = n // 2
        kv, kv1, qr, os, ls = (bufs[nm, l] for nm in ("kv", "kv1", "qr", "os", "ls"))
        kv1[...] = kv[...] * high_b + low_b

        def body(it, _):
            i = lax.rem(it + 1, heads)
            x = qr[i].astype(F32) * scale
            qa = jnp.where(low, x, 0.0).astype(BF)
            qb = jnp.where(low, half_roll(x), 0.0).astype(BF)
            if h >= LANES:
                oa, ma = attention(qa, kv[...], kv1[...])
                ob, mb = attention(qb, kv[...], kv1[...])
                o = None
            else:
                o, m = attention(jnp.concatenate([qa, qb], axis=0), kv[...], kv1[...])
                oa, ob, ma, mb = o[:h], o[h:], m[:h], m[h:]
            ya, yb = oa / half_roll(oa), ob / half_roll(ob)
            os[i] = jnp.where(low, half_roll(ya), yb).astype(BF)
            la = ma + jnp.log(jnp.where(low, oa, 1.0))
            lb = mb + jnp.log(jnp.where(low, ob, 1.0))
            parts = [la, lb]
            if n < LANES:
                parts.append(jnp.zeros((LANES - n, LANES), F32))
            ls[i] = jnp.concatenate(parts, axis=0).T[0:8, :]

            @pl.when(it < heads - 1)
            def _():
                for c in copies_back(l, i, mine):
                    c.start()

            return 0

        lax.fori_loop(0, heads, body, 0)
        bufs["ro", l][mine] = os[0]
        bufs["rl", l][mine] = ls[0]

    def unpack(l):
        n = counts[l]
        h = n // 2
        for i in range(1, heads):
            for c in copies_back(l, i, flip(mine, i, gbits)):
                c.wait_recv()
        ro, rl = bufs["ro", l], bufs["rl", l]
        for p in range(pairs):
            cut = slice(p * LANES, (p + 1) * LANES)
            a, b = halves(ro[2 * p].astype(F32), ro[2 * p + 1].astype(F32))
            out_buf[0:h, cut] = a.astype(BF)
            out_buf[h:n, cut] = b.astype(BF)
            for c in range(max(n // LANES, 1)):
                m = min(n, LANES)
                cc = slice(c * LANES, (c + 1) * LANES)
                x0 = jnp.broadcast_to(rl[2 * p, 0:1, cc], (LANES // 2, LANES))
                x1 = jnp.broadcast_to(rl[2 * p + 1, 0:1, cc], (LANES // 2, LANES))
                e = jnp.concatenate([x0, x1], axis=0).T
                lse_buf[c * m : (c + 1) * m, cut] = e[0:m]

    for l in (2, 4, 3):
        arrive(l)
        if l == 2:
            work(2)
            continue
        for b in range(fars[l]):
            c = copy_far(l, b)
            c.start()
            c.wait_recv()
        work(l)

    for l in (2, 4, 3):
        unpack(l)
        merge(l, rates[l], out_buf, l == 3)

    for l in levels:
        for i in range(1, heads):
            for c in copies_in(l, i) + copies_back(l, i, mine):
                c.wait_send()
        for b in range(fars[l]):
            copy_far(l, b).wait_send()


def per_device(places, query, key, value, offsets):
    rows, width = query.shape
    heads = offsets.shape[1]
    size = width // heads
    rate3 = RATE1 * places // 8
    rates = {2: RATE1, 3: rate3, 4: 4 * rate3}
    counts = {l: rows // r for l, r in rates.items()}
    group_bits = heads.bit_length() - 1
    bits = places.bit_length() - 1
    fars = {2: 0, 3: bits - 1 - group_bits, 4: bits - group_bits}
    spread = jnp.repeat(offsets.astype(jnp.int32), size, axis=1)
    spread = jnp.pad(spread, ((0, 8 - spread.shape[0]), (0, 0)))
    scratch = []
    for l in (2, 3, 4):
        n = counts[l]
        keys = heads * n << fars[l]
        scratch += [
            pltpu.VMEM((heads, n // 2, LANES), BF),
            pltpu.VMEM((heads, n, LANES), BF),
            pltpu.VMEM((heads, n // 2, LANES), BF),
            pltpu.VMEM((keys, LANES), BF),
            pltpu.VMEM((keys, LANES), BF),
            pltpu.VMEM((heads, n // 2, LANES), BF),
            pltpu.VMEM((heads, 8, max(n, LANES)), F32),
            pltpu.VMEM((heads, n // 2, LANES), BF),
            pltpu.VMEM((heads, 8, max(n, LANES)), F32),
        ]
    few = rows // RATE1
    scratch += [pltpu.VMEM((few, width), BF)] * 3
    scratch += [pltpu.VMEM((few, width), F32)] * 2
    scratch += [pltpu.VMEM((few, width), BF)]
    scratch += [pltpu.VMEM((rows, width), F32)] * 3
    scratch += [pltpu.SemaphoreType.DMA((3, heads))] * 8
    scratch += [pltpu.SemaphoreType.DMA((3, max(fars[4], 1)))] * 2
    cfg = (rates, counts, fars, heads, rows, width)
    return pl.pallas_call(
        functools.partial(kernel, cfg),
        out_shape=jax.ShapeDtypeStruct((rows, width), BF),
        in_specs=[pl.BlockSpec(memory_space=pltpu.VMEM)] * 4,
        out_specs=pl.BlockSpec(memory_space=pltpu.VMEM),
        scratch_shapes=scratch,
        compiler_params=pltpu.CompilerParams(
            collective_id=0, has_side_effects=True, vmem_limit_bytes=48 * 1024 * 1024
        ),
    )(query, key, value, spread)


def solution(mesh):
    return jax.shard_map(
        functools.partial(per_device, mesh.shape["seq"]),
        mesh=mesh,
        in_specs=(P("seq", "head"), P("seq", "head"), P("seq", "head"), P(None, "head")),
        out_specs=P("seq", "head"),
        check_vma=False,
    )
```

profile of v0, /device:TPU:0, one launch (start us, length us, event | category | flops | bytes accessed | tf_op | source)
XLA Modules:
  0.0 64.2 jit_solution(2050855761002154416)
XLA Ops:
  0.0 0.8 %copy.5 = s32[5,4]{1,0:T(8,128)S(1)} copy(s32[5,4]{0,1:T(4,128)} %param.7) | data formatting | bytes 160 | tf_op args[3]
  0.8 0.1 broadcast_in_dim.3
  0.8 0.1 reshape.3
  0.9 0.0 copy-start
  0.9 1.2 %copy-done = bf16[2048,256]{1,0:T(8,128)(2,1)S(1)} copy-done((bf16[2048,256]{1,0:T(8,128)(2,1)S(1)}, bf16[2048,256]{1,0:T(8,128)(2,1)}, u32[]{:S(2)}) %copy-start) | copy-done | bytes 1048600
  2.2 0.0 copy-start.1
  2.2 1.2 %copy-done.1 = bf16[2048,256]{1,0:T(8,128)(2,1)S(1)} copy-done((bf16[2048,256]{1,0:T(8,128)(2,1)S(1)}, bf16[2048,256]{1,0:T(8,128)(2,1)}, u32[]{:S(2)}) %copy-start.1) | copy-done | bytes 1048600
  3.4 0.0 copy-start.2
  3.4 1.2 %copy-done.2 = bf16[2048,256]{1,0:T(8,128)(2,1)S(1)} copy-done((bf16[2048,256]{1,0:T(8,128)(2,1)S(1)}, bf16[2048,256]{1,0:T(8,128)(2,1)}, u32[]{:S(2)}) %copy-start.2) | copy-done | bytes 1048600
  4.6 58.6 %shard_map.46 = bf16[2048,256]{1,0:T(8,128)(2,1)S(1)} custom-call(bf16[2048,256]{1,0:T(8,128)(2,1)S(1)} %copy-done, bf16[2048,256]{1,0:T(8,128)(2,1)S(1)} %copy-done.1, bf16[2048,256]{1,0:T(8,128)(2,1)S(1)} %copy-done.2, s32[8,256]{1,0:T(8,128)S(1)} %pad.4.offs_ref), custom_call_target="tpu_custom_call" | custom-call | tf_op jit(solution)/shard_map/pallas_call | solution.py:387
  63.2 1.0 %copy.7 = bf16[2048,256]{1,0:T(8,128)(2,1)} copy(bf16[2048,256]{1,0:T(8,128)(2,1)S(1)} %shard_map.46) | data formatting | bytes 2097152
  (1 shorter events, 0.0 us)
Async XLA Ops:
  0.9 1.2 %copy-start = (bf16[2048,256]{1,0:T(8,128)(2,1)S(1)}, bf16[2048,256]{1,0:T(8,128)(2,1)}, u32[]{:S(2)}) copy-start(bf16[2048,256]{1,0:T(8,128)(2,1)} %q_ref.1) | copy-start | bytes 3145732
  2.2 1.2 %copy-start.1 = (bf16[2048,256]{1,0:T(8,128)(2,1)S(1)}, bf16[2048,256]{1,0:T(8,128)(2,1)}, u32[]{:S(2)}) copy-start(bf16[2048,256]{1,0:T(8,128)(2,1)} %k_ref.1) | copy-start | bytes 3145732
  3.4 1.2 %copy-start.2 = (bf16[2048,256]{1,0:T(8,128)(2,1)S(1)}, bf16[2048,256]{1,0:T(8,128)(2,1)}, u32[]{:S(2)}) copy-start(bf16[2048,256]{1,0:T(8,128)(2,1)} %v_ref.1) | copy-start | bytes 3145732
where the time goes:
time: 64.4 us; the launch traced here: 64.2 us
  Pallas kernels  58.6 us (91%)
  local copies, waits for them, and re-layouts  5.58 us (9%)
    pallas_call x1, Pallas kernels, per_device(): pl.pallas_call(functools.partial(kernel, cfg), out_shape=jax.ShapeDtypeSt...  58.6 us
    unnamed x8, local copies, waits for them, and re-layouts  5.42 us

commit v1 on v0

--- a/solution.py
+++ b/solution.py
@@ -49,17 +49,24 @@
     return dot(p, v_one), top
 
 
-def kernel(cfg, q_ref, k_ref, v_ref, offs_ref, out_ref, *scratch):
+def kernel(cfg, q_hbm, k_hbm, v_hbm, offs_ref, out_ref, *scratch):
     rates, counts, fars, heads, rows, width = cfg
     levels = (2, 3, 4)
-    names = ("qs", "kvs", "qr", "kv", "kv1", "os", "ls", "ro", "rl")
+    all_rates = {1: RATE1, **rates}
+    names = ("qs", "kvs", "qr", "kv", "kv1", "os", "ls", "ro", "rl", "out", "lse")
+    loads = []
     bufs = {}
     pos = 0
     for l in levels:
         for nm in names:
             bufs[nm, l] = scratch[pos]
             pos += 1
-    (q1, k1, v1, out_l1, lse_buf, out_buf, num, tot, mx, sq, rq, skv, rkv, so, ro_s, sl, rl_s, sfar, rfar) = scratch[pos:]
+    (q_ref, k_ref, v_ref, sin, q1, k1, v1, out_l1, lse_l1, num, tot, mx, sq, rq, skv, rkv, so, ro_s, sl, rl_s, sfar, rfar) = scratch[pos:]
+
+    bufs["out", 1], bufs["lse", 1] = out_l1, lse_l1
+    for x, (a, b) in enumerate(((q_hbm, q_ref), (k_hbm, k_ref), (v_hbm, v_ref))):
+        loads.append(pltpu.make_async_copy(a, b, sin.at[x]))
+        loads[-1].start()
 
     me = lax.axis_index("seq")
     hd = lax.axis_index("head")
@@ -101,7 +108,11 @@
 
     def hits(l, rate, tile):
         r = lax.broadcasted_iota(jnp.int32, (tile, width), 0) & (rate - 1)
-        return r == offs_ref[l : l + 1, :]
+        lane = lax.broadcasted_iota(jnp.int32, (1, width), 1)
+        want = jnp.full((1, width), offs_ref[l, 0], jnp.int32)
+        for h in range(1, heads):
+            want = jnp.where(lane >= h * (width // heads), offs_ref[l, h], want)
+        return r == want
 
     def halves(a, b):
         return jnp.where(low, a, half_roll(b)), jnp.where(low, half_roll(a), b)
@@ -167,6 +178,8 @@
             src_ref=bufs["kv", l].at[pl.ds(0, n)], dst_ref=bufs["kv", l].at[pl.ds(n, n)],
             send_sem=sfar.at[l - 2, b], recv_sem=rfar.at[l - 2, b], device_id=far_dev(b), device_id_type=MESH)
 
+    for c in loads:
+        c.wait()
     first = True
     for l in (2, 4, 3):
         pack(l)
@@ -188,7 +201,7 @@
             jnp.where(low, m0, m1),
         )
 
-    qt = SEG // 2
+    qt = SEG
 
     def first_level(t, _):
         at = pl.ds(pl.multiple_of(t * qt, qt), qt)
@@ -219,38 +232,45 @@
             cut = slice(p * LANES, (p + 1) * LANES)
             a, b, c = pair_attention(q1[at, cut], k1[:, cut], v1[:, cut])
             out_l1[at, cut] = a / b
-            lse_buf[at, cut] = c + jnp.log(b)
+            lse_l1[at, cut] = c + jnp.log(b)
         return 0
 
     lax.fori_loop(0, rows // RATE1 // qt, second_level, 0)
 
-    def merge(l, rate, source, last):
-        tile = tile_of(rate)
-        g = tile // rate
-        fine = source.dtype == F32
-        s_out = spreader(rate, tile, 2 if fine else 1)
-        s_lse = spreader(rate, tile, 3)
-        hit = hits(l, rate, tile)
+    def merge(which, last):
+        tile = max(tile_of(all_rates[l]) for l in which)
+        fixed = {}
+        for l in which:
+            rate = all_rates[l]
+            fine = bufs["out", l].dtype == F32
+            fixed[l] = (spreader(rate, tile, 2 if fine else 1), spreader(rate, tile, 3), hits(l, rate, tile), fine)
 
         def body(t, _):
             at = pl.ds(pl.multiple_of(t * tile, tile), tile)
-            pt = pl.ds(pl.multiple_of(t * g, g), g)
-            o = source[pt, :]
-            if fine:
-                hi = o.astype(BF).astype(F32)
-                o = jnp.concatenate([hi, o - hi], axis=0).astype(BF)
-            e = lse_buf[pt, :]
-            e0 = e.astype(BF).astype(F32)
-            e1 = (e - e0).astype(BF).astype(F32)
-            e2 = e - e0 - e1
-            x = dot(s_out, o)
-            y = dot(s_lse, jnp.concatenate([e0, e1, e2], axis=0).astype(BF))
-            y = jnp.where(hit, y, NEG)
-            old = mx[at, :]
-            new = jnp.maximum(old, y)
-            a, b = jnp.exp(old - new), jnp.exp(y - new)
-            nn = num[at, :] * a + x * b
-            tt = tot[at, :] * a + b
+            found = []
+            old = new = mx[at, :]
+            for l in which:
+                s_out, s_lse, hit, fine = fixed[l]
+                g = tile // all_rates[l]
+                pt = pl.ds(pl.multiple_of(t * g, g), g)
+                o = bufs["out", l][pt, :]
+                if fine:
+                    hi = o.astype(BF).astype(F32)
+                    o = jnp.concatenate([hi, o - hi], axis=0).astype(BF)
+                e = bufs["lse", l][pt, :]
+                e0 = e.astype(BF).astype(F32)
+                e1 = (e - e0).astype(BF).astype(F32)
+                e2 = e - e0 - e1
+                x = dot(s_out, o)
+                y = dot(s_lse, jnp.concatenate([e0, e1, e2], axis=0).astype(BF))
+                y = jnp.where(hit, y, NEG)
+                new = jnp.maximum(new, y)
+                found.append((x, y))
+            a = jnp.exp(old - new)
+            nn, tt = num[at, :] * a, tot[at, :] * a
+            for x, y in found:
+                b = jnp.exp(y - new)
+                nn, tt = nn + x * b, tt + b
             if last:
                 out_ref[at, :] = (nn / tt).astype(BF)
             else:
@@ -261,7 +281,7 @@
 
         lax.fori_loop(0, rows // tile, body, 0)
 
-    merge(1, RATE1, out_l1, False)
+    merge((1,), False)
 
     def arrive(l):
         for i in range(1, heads):
@@ -279,13 +299,8 @@
             x = qr[i].astype(F32) * scale
             qa = jnp.where(low, x, 0.0).astype(BF)
             qb = jnp.where(low, half_roll(x), 0.0).astype(BF)
-            if h >= LANES:
-                oa, ma = attention(qa, kv[...], kv1[...])
-                ob, mb = attention(qb, kv[...], kv1[...])
-                o = None
-            else:
-                o, m = attention(jnp.concatenate([qa, qb], axis=0), kv[...], kv1[...])
-                oa, ob, ma, mb = o[:h], o[h:], m[:h], m[h:]
+            o, m = attention(jnp.concatenate([qa, qb], axis=0), kv[...], kv1[...])
+            oa, ob, ma, mb = o[:h], o[h:], m[:h], m[h:]
             ya, yb = oa / half_roll(oa), ob / half_roll(ob)
             os[i] = jnp.where(low, half_roll(ya), yb).astype(BF)
             la = ma + jnp.log(jnp.where(low, oa, 1.0))
@@ -312,7 +327,7 @@
         for i in range(1, heads):
             for c in copies_back(l, i, flip(mine, i, gbits)):
                 c.wait_recv()
-        ro, rl = bufs["ro", l], bufs["rl", l]
+        ro, rl, out_buf, lse_buf = (bufs[nm, l] for nm in ("ro", "rl", "out", "lse"))
         for p in range(pairs):
             cut = slice(p * LANES, (p + 1) * LANES)
             a, b = halves(ro[2 * p].astype(F32), ro[2 * p + 1].astype(F32))
@@ -337,9 +352,11 @@
             c.wait_recv()
         work(l)
 
-    for l in (2, 4, 3):
-        unpack(l)
-        merge(l, rates[l], out_buf, l == 3)
+    unpack(2)
+    unpack(4)
+    merge((2, 4), False)
+    unpack(3)
+    merge((3,), True)
 
     for l in levels:
         for i in range(1, heads):
@@ -359,8 +376,6 @@
     group_bits = heads.bit_length() - 1
     bits = places.bit_length() - 1
     fars = {2: 0, 3: bits - 1 - group_bits, 4: bits - group_bits}
-    spread = jnp.repeat(offsets.astype(jnp.int32), size, axis=1)
-    spread = jnp.pad(spread, ((0, 8 - spread.shape[0]), (0, 0)))
     scratch = []
     for l in (2, 3, 4):
         n = counts[l]
@@ -375,11 +390,13 @@
             pltpu.VMEM((heads, 8, max(n, LANES)), F32),
             pltpu.VMEM((heads, n // 2, LANES), BF),
             pltpu.VMEM((heads, 8, max(n, LANES)), F32),
+            pltpu.VMEM((n, width), BF),
+            pltpu.VMEM((n, width), F32),
         ]
     few = rows // RATE1
+    scratch += [pltpu.VMEM((rows, width), BF)] * 3 + [pltpu.SemaphoreType.DMA((3,))]
     scratch += [pltpu.VMEM((few, width), BF)] * 3
     scratch += [pltpu.VMEM((few, width), F32)] * 2
-    scratch += [pltpu.VMEM((few, width), BF)]
     scratch += [pltpu.VMEM((rows, width), F32)] * 3
     scratch += [pltpu.SemaphoreType.DMA((3, heads))] * 8
     scratch += [pltpu.SemaphoreType.DMA((3, max(fars[4], 1)))] * 2
@@ -387,13 +404,13 @@
     return pl.pallas_call(
         functools.partial(kernel, cfg),
         out_shape=jax.ShapeDtypeStruct((rows, width), BF),
-        in_specs=[pl.BlockSpec(memory_space=pltpu.VMEM)] * 4,
+        in_specs=[pl.BlockSpec(memory_space=pl.ANY)] * 3 + [pl.BlockSpec(memory_space=pltpu.SMEM)],
         out_specs=pl.BlockSpec(memory_space=pltpu.VMEM),
         scratch_shapes=scratch,
         compiler_params=pltpu.CompilerParams(
             collective_id=0, has_side_effects=True, vmem_limit_bytes=48 * 1024 * 1024
         ),
-    )(query, key, value, spread)
+    )(query, key, value, offsets)
 
 
 def solution(mesh):

time: 64.4 us -> 65 us (level)
  Pallas kernels: 58.6 us -> 59.3 us
    pallas_call x1, Pallas kernels: 58.6 us -> 59.3 us  [per_device(): pl.pallas_call(functools.partial(kernel, cfg), out_shape=jax.ShapeDtypeSt...]
where the time goes in v1:
time: 65 us; the launch traced here: 64.7 us
  Pallas kernels  59.3 us (91%)
  local copies, waits for them, and re-layouts  5.41 us (8%)
    pallas_call x1, Pallas kernels, per_device(): pl.pallas_call(functools.partial(kernel, cfg), out_shape=jax.ShapeDtypeSt...  59.3 us
    unnamed x8, local copies, waits for them, and re-layouts  5.41 us

profile of v1, /device:TPU:0, one launch (start us, length us, event | category | flops | bytes accessed | tf_op | source)
XLA Modules:
  0.0 64.7 jit_solution(887803390594868228)
XLA Ops:
  0.0 0.8 %copy.5.offs_ref = s32[5,4]{1,0:T(8,128)S(1)} copy(s32[5,4]{0,1:T(4,128)} %param.7) | data formatting | bytes 160 | tf_op args[3]
  0.8 0.0 copy-start
  0.8 1.2 %copy-done = bf16[2048,256]{1,0:T(8,128)(2,1)S(1)} copy-done((bf16[2048,256]{1,0:T(8,128)(2,1)S(1)}, bf16[2048,256]{1,0:T(8,128)(2,1)}, u32[]{:S(2)}) %copy-start) | copy-done | bytes 1048600
  2.0 0.0 copy-start.1
  2.0 1.2 %copy-done.1 = bf16[2048,256]{1,0:T(8,128)(2,1)S(1)} copy-done((bf16[2048,256]{1,0:T(8,128)(2,1)S(1)}, bf16[2048,256]{1,0:T(8,128)(2,1)}, u32[]{:S(2)}) %copy-start.1) | copy-done | bytes 1048600
  3.2 0.0 copy-start.2
  3.2 1.2 %copy-done.2 = bf16[2048,256]{1,0:T(8,128)(2,1)S(1)} copy-done((bf16[2048,256]{1,0:T(8,128)(2,1)S(1)}, bf16[2048,256]{1,0:T(8,128)(2,1)}, u32[]{:S(2)}) %copy-start.2) | copy-done | bytes 1048600
  4.4 59.3 %shard_map.46 = bf16[2048,256]{1,0:T(8,128)(2,1)S(1)} custom-call(bf16[2048,256]{1,0:T(8,128)(2,1)S(1)} %copy-done, bf16[2048,256]{1,0:T(8,128)(2,1)S(1)} %copy-done.1, bf16[2048,256]{1,0:T(8,128)(2,1)S(1)} %copy-done.2, s32[5,4]{1,0:T(8,128)S(1)} %copy.5.offs_ref), custom_call_target="tpu_custom_call" | custom-call | tf_op jit(solution)/shard_map/pallas_call | solution.py:404
  63.8 1.0 %copy.7 = bf16[2048,256]{1,0:T(8,128)(2,1)} copy(bf16[2048,256]{1,0:T(8,128)(2,1)S(1)} %shard_map.46) | data formatting | bytes 2097152
Async XLA Ops:
  0.8 1.2 %copy-start = (bf16[2048,256]{1,0:T(8,128)(2,1)S(1)}, bf16[2048,256]{1,0:T(8,128)(2,1)}, u32[]{:S(2)}) copy-start(bf16[2048,256]{1,0:T(8,128)(2,1)} %q_hbm.1) | copy-start | bytes 3145732
  2.0 1.2 %copy-start.1 = (bf16[2048,256]{1,0:T(8,128)(2,1)S(1)}, bf16[2048,256]{1,0:T(8,128)(2,1)}, u32[]{:S(2)}) copy-start(bf16[2048,256]{1,0:T(8,128)(2,1)} %k_hbm.1) | copy-start | bytes 3145732
  3.2 1.2 %copy-start.2 = (bf16[2048,256]{1,0:T(8,128)(2,1)S(1)}, bf16[2048,256]{1,0:T(8,128)(2,1)}, u32[]{:S(2)}) copy-start(bf16[2048,256]{1,0:T(8,128)(2,1)} %v_hbm.1) | copy-start | bytes 3145732
